TPU v7x, 256 devices: a whole 4x4x8 slice. The times are simulated.
256 devices in a mesh: gx: 16 (over y, x), gy: 16 (over z, core).
Axes of the slice: x: 4, y: 4, z: 8, core: 2. Of those that a mesh axis runs over, the one named last changes fastest.
Arguments:
- pressure: float32 [2, 2048, 2048], P(None, 'gx', 'gy'), may hold values from 0.5 to 1.5
- saturations: float32 [2, 2, 2048, 2048], P(None, None, 'gx', 'gy'), may hold values from 0.05 to 0.4
- old_mass: float32 [3, 2, 2048, 2048], P(None, None, 'gx', 'gy'), may hold values from 0 to 0.4
- pore_volume: float32 [2, 2048, 2048], P(None, 'gx', 'gy'), may hold values from 0.3 to 3
- transmissibility: float32 [3, 2, 2048, 2048], P(None, None, 'gx', 'gy'), may hold values from 0.3 to 3
- direction: float32 [3, 2, 2048, 2048], P(None, None, 'gx', 'gy'), may hold values from -6 to 6
- seg_pressure: float32 [512, 128], P('gx'), may hold values from 0.4 to 1.2
- seg_direction: float32 [512, 128], P('gx'), may hold values from -6 to 6
- perf_cell: int32 [512, 128], P('gx'), may hold values from 0 to 524287, as said below
- well_index: float32 [512, 128], P('gx'), may hold values from 0.2 to 2
- parent: int32 [512, 128], P('gx'), may hold values from 0 to 126, as said below
- seg_head: float32 [512, 128], P('gx'), may hold values from 0 to 0.3
- well_mode: int32 [512], P('gx'), may hold values from 0 to 1
- bhp_limit: float32 [512], P('gx'), may hold values from 0.3 to 0.8
- guide_rate: float32 [512], P('gx'), may hold values from 0.5 to 5
- group_of: int32 [512, 1], P('gx'), may hold values from 0 to 127
- group_target: float32 [128], replicated, may hold values from 200 to 800
Outputs:
- cell_residual: float32 [3, 2, 2048, 2048], P(None, None, 'gx', 'gy')
- cell_jvp: float32 [3, 2, 2048, 2048], P(None, None, 'gx', 'gy')
- seg_residual: float32 [512, 128], P(('gx', 'gy'))
- seg_jvp: float32 [512, 128], P(('gx', 'gy'))
- group_rates: float32 [3, 128], replicated
Inputs may be any that keep to these rules, and one draw needn't show every extreme that they name: perf_cell codes (layer * 128 + xl) * 2048 + row, with xl the column within the strip of 128 columns of the well's block of 32 wells. `parent`: segment 0 of every well names itself; every other segment names a segment of lower number. `group_of`: every group has at least one well.
All inputs are finite; a program needn't handle non-finite values.
Results may differ from a plain program's by a relative error of at most 0.0003.
Values sent between devices are 32-bit elements; how exact they have to be, the bound alone decides.
A program may use at most 128 MiB of HBM per device.

v0:
```python
import jax
import jax.numpy as jnp
from jax import lax
from jax.sharding import PartitionSpec as P

COMPRESS = (0.05, 0.2, 1.0)
VISCOSITY = (0.5, 1.0, 0.2)
DENSITY = (1.0, 0.8, 0.2)
ROCK_COMP = 0.01
GRAVITY = 0.05
UPWIND_WIDTH = 0.02
FRICTION = 0.002
RATE_SCALE = 0.1


def padded_2(x, sides, width):
    for axis, dim in sides:
        devices, length = (lax.axis_size(axis), x.shape[dim])
        up = [(i, (i + 1) % devices) for i in range(devices - 1)]
        down = [(j, i) for i, j in up]
        last = lax.slice_in_dim(x, length - width, length, axis=dim)
        first = lax.slice_in_dim(x, 0, width, axis=dim)
        before = lax.ppermute(last, axis, up)
        after = lax.ppermute(first, axis, down)
        x = jnp.concatenate([before, x, after], axis=dim)
    return x


def phase_props(press, water, gas):
    oil = 1.0 - water - gas
    satur = (water, oil, gas)
    rock = 1.0 + ROCK_COMP * (press - 1.0)
    mobility = []
    masses = []
    for phase in range(3):
        volume = jnp.exp(COMPRESS[phase] * (press - 1.0))
        mobility.append(satur[phase] * satur[phase] * volume / VISCOSITY[phase])
        masses.append(rock * satur[phase] * volume)
    return (jnp.stack(mobility), jnp.stack(masses))


def face_flux(press_in, press_out, mobil_in, mobil_out, trans, lift):
    fluxes = []
    for phase in range(3):
        potential = press_in - press_out + DENSITY[phase] * lift
        upwind = jax.nn.sigmoid(potential / UPWIND_WIDTH)
        fluxes.append(
            trans * (upwind * mobil_in[phase] + (1.0 - upwind) * mobil_out[phase]) * potential
        )
    return jnp.stack(fluxes)


def ancestry(parent):
    count = parent.shape[1]
    segment_ids = jnp.arange(count, dtype=jnp.int32)
    reach = (segment_ids[None, :, None] == segment_ids[None, None, :]) | (
        parent[:, None, :] == segment_ids[None, :, None]
    )
    reach = reach.astype(jnp.bfloat16)
    for level in range((count - 1).bit_length()):
        product = jnp.einsum("wsu,wut->wst", reach, reach, preferred_element_type=jnp.float32)
        reach = jnp.minimum(product, 1.0).astype(jnp.bfloat16)
    return reach.astype(jnp.float32)


def segment_terms(parent, seg_head, well_mode, bhp_limit, target):
    reach = ancestry(parent)

    def equations(total_vals, seg_vals):
        flow = jnp.einsum("wst,wt->ws", reach, total_vals, precision=lax.Precision.HIGHEST)
        above = jnp.take_along_axis(seg_vals, parent, axis=1)
        inner = seg_vals - above - seg_head - FRICTION * flow
        root = jnp.where(
            well_mode == 1, RATE_SCALE * (flow[:, 0] - target), seg_vals[:, 0] - bhp_limit
        )
        return inner.at[:, 0].set(root)

    return equations


def per_device(
    pressure,
    saturations,
    old_mass,
    pore_volume,
    transmissibility,
    direction,
    seg_pressure,
    seg_direction,
    perf_cell,
    well_index,
    parent,
    seg_head,
    well_mode,
    bhp_limit,
    guide_rate,
    group_of,
    group_target,
):
    layers, cols, rows = pressure.shape
    col_count = lax.axis_size("gx")
    row_count = lax.axis_size("gy")
    col_index = lax.axis_index("gx")
    row_index = lax.axis_index("gy")
    col_glob = col_index * cols + jnp.arange(cols, dtype=jnp.int32)
    row_glob = row_index * rows + jnp.arange(rows, dtype=jnp.int32)
    trans_cols = jnp.where(
        (col_glob == cols * col_count - 1)[None, :, None], 0.0, transmissibility[0]
    )
    trans_rows = jnp.where(
        (row_glob == rows * row_count - 1)[None, None, :], 0.0, transmissibility[1]
    )
    stacked = jnp.concatenate(
        [pressure[None], saturations, direction, trans_cols[None], trans_rows[None]], axis=0
    )
    padded = padded_2(stacked, (("gx", 2), ("gy", 3)), 1)
    state_pad = padded[0:3]
    direc_pad = padded[3:6]
    tcol_pad = padded[6]
    trow_pad = padded[7]
    all_rows = rows * row_count
    layer_span = cols * all_rows
    layer = perf_cell // layer_span
    remain = perf_cell % layer_span
    local_row = remain % all_rows - row_index * rows
    owned = (local_row >= 0) & (local_row < rows)
    flat_cell = (layer * cols + remain // all_rows) * rows + jnp.clip(local_row, 0, rows - 1)
    weight = jnp.where(owned, well_index, 0.0)

    def local_terms(state, seg_vals):
        press = state[0]
        mobility, masses = phase_props(press, state[1], state[2])
        mobil_in = mobility[:, :, 1:-1, 1:-1]
        press_in = press[:, 1:-1, 1:-1]
        residual = masses[:, :, 1:-1, 1:-1] * pore_volume - old_mass
        flux_cols = face_flux(
            press[:, :-1, 1:-1],
            press[:, 1:, 1:-1],
            mobility[:, :, :-1, 1:-1],
            mobility[:, :, 1:, 1:-1],
            tcol_pad[:, :-1, 1:-1],
            0.0,
        )
        residual = residual + flux_cols[:, :, 1:] - flux_cols[:, :, :-1]
        flux_rows = face_flux(
            press[:, 1:-1, :-1],
            press[:, 1:-1, 1:],
            mobility[:, :, 1:-1, :-1],
            mobility[:, :, 1:-1, 1:],
            trow_pad[:, 1:-1, :-1],
            0.0,
        )
        residual = residual + flux_rows[:, :, :, 1:] - flux_rows[:, :, :, :-1]
        flux_layers = face_flux(
            press_in[:-1],
            press_in[1:],
            mobil_in[:, :-1],
            mobil_in[:, 1:],
            transmissibility[2][:-1],
            GRAVITY,
        )
        residual = (
            residual
            + jnp.pad(flux_layers, ((0, 0), (0, 1), (0, 0), (0, 0)))
            - jnp.pad(flux_layers, ((0, 0), (1, 0), (0, 0), (0, 0)))
        )
        mobil_flat = mobil_in.reshape(3, -1)
        rates = weight * mobil_flat[:, flat_cell] * (press_in.reshape(-1)[flat_cell] - seg_vals)
        residual = (
            residual.reshape(3, -1)
            .at[:, flat_cell.reshape(-1)]
            .add(rates.reshape(3, -1))
            .reshape(residual.shape)
        )
        return (residual, rates)

    primal, tangent = jax.jvp(local_terms, (state_pad, seg_pressure), (direc_pad, seg_direction))
    cell_residual, rates = primal
    cell_jvp, rate_tangent = tangent
    rate_total = jnp.sum(rates, axis=0)
    total_tangent = jnp.sum(rate_tangent, axis=0)
    member = (
        group_of[:, 0][:, None] == jnp.arange(group_target.shape[0], dtype=jnp.int32)[None, :]
    ).astype(jnp.float32)
    rates_part = jnp.dot(jnp.sum(rates, axis=2), member, precision=lax.Precision.HIGHEST)
    guide_part = jnp.dot(guide_rate, member, precision=lax.Precision.HIGHEST)
    guide_total = lax.psum(guide_part, "gx")
    group_rates = lax.psum(rates_part, ("gx", "gy"))
    target = (
        jnp.dot(member, group_target, precision=lax.Precision.HIGHEST)
        * guide_rate
        / jnp.dot(member, guide_total, precision=lax.Precision.HIGHEST)
    )
    well_count = seg_pressure.shape[0]
    share = well_count // row_count
    start = row_index * share

    def pick(values):
        return lax.dynamic_slice_in_dim(values, start, share, 0)

    total_sum, tangent_sum = lax.psum((rate_total, total_tangent), "gy")
    equations = segment_terms(parent, seg_head, well_mode, bhp_limit, target)
    seg_full, seg_tan = jax.jvp(equations, (total_sum, seg_pressure), (tangent_sum, seg_direction))
    seg_residual = pick(seg_full)
    seg_jvp = pick(seg_tan)
    return (cell_residual, cell_jvp, seg_residual, seg_jvp, group_rates)


def solution(mesh):
    placed = (
        P(None, "gx", "gy"),
        P(None, None, "gx", "gy"),
        P(None, None, "gx", "gy"),
        P(None, "gx", "gy"),
        P(None, None, "gx", "gy"),
        P(None, None, "gx", "gy"),
        P("gx", None),
        P("gx", None),
        P("gx", None),
        P("gx", None),
        P("gx", None),
        P("gx", None),
        P("gx"),
        P("gx"),
        P("gx"),
        P("gx", None),
        P(),
    )
    return jax.shard_map(
        per_device,
        mesh=mesh,
        in_specs=placed,
        out_specs=(
            P(None, None, "gx", "gy"),
            P(None, None, "gx", "gy"),
            P(("gx", "gy"), None),
            P(("gx", "gy"), None),
            P(),
        ),
        check_vma=False,
    )
```

profile of v0, /device:TPU:1, one launch (start us, length us, event | category | flops | bytes accessed | tf_op | source)
XLA Modules:
  0.0 510.7 jit_solution(14686973665699037031)
XLA Ops:
  6.9 4.6 collective-permute-start
  15.0 2.0 minimum_convert_fusion
  17.2 32.3 %psum.29 = f32[128]{0:T(128)S(1)} all-reduce(f32[128]{0:T(128)S(1)} %convolution_bitcast_fusion.1), channel_id=1, replica_groups=mesh['gx'=16,'gy'=16] {'gx'}, use_global_device_ids=true, to_apply=%region_5.6 | all-reduce | flops 128 | bytes 1024 | tf_op jit(solution)/shard_map/psum | solution.py:187
  51.9 9.9 %collective-permute-start.3 = (f32[8,2,130,1]{2,0,3,1:T(8,128)S(1)}, f32[8,2,130,1]{2,0,3,1:T(8,128)S(1)}, u32[]{:S(2)}, u32[]{:S(2)}) collective-permute-start(f32[8,2,130,1]{2,0,3,1:T(8,128)S(1)} %copy.106), channel_id=1, source_target_pairs={{1,0},{2,1},{3,2},{4,3},{5,4},{6,5},{7,6},{8,7},{9,8},{10,9},{11,1... | collective-permute-start | bytes 24968 | tf_op jit(solution)/shard_map/ppermute | solution.py:24
  62.4 3.6 collective-permute-start.2
  66.2 43.2 %gather_fusion.5 = f32[4096]{0:T(1024)} fusion(f32[32,128]{1,0:T(8,128)S(1)} %copy-done.1, s32[4096]{0:T(1024)S(1)} %fusion.156), kind=kCustom, calls=%fused_computation.5 | custom fusion | bytes 65536 | tf_op jit(solution)/shard_map/jvp(jit(take_along_axis))/gather | solution.py:71
  109.4 25.6 %gather_fusion.4 = f32[4096]{0:T(1024)S(1)} fusion(f32[32,128]{1,0:T(8,128)S(1)} %copy-done.2, s32[4096]{0:T(1024)S(1)} %fusion.156), kind=kCustom, calls=%fused_computation.4 | custom fusion | bytes 65536 | tf_op jit(solution)/shard_map/jvp(jit(take_along_axis))/gather | solution.py:71
  145.2 8.6 %copy.109 = f32[3,2,128,128]{0,3,2,1:T(8,128)} copy(f32[3,2,128,128]{3,2,1,0:T(8,128)S(1)} %fusion.34) | data formatting | bytes 786432 | tf_op jit(solution)/shard_map/jvp()/sub | solution.py:163
  153.7 8.5 %copy.110 = f32[3,2,128,128]{0,3,2,1:T(8,128)} copy(f32[3,2,128,128]{3,2,1,0:T(8,128)S(1)} %get-tuple-element.106) | data formatting | bytes 786432 | tf_op jit(solution)/shard_map/jvp()/slice | solution.py:133
  162.2 16.5 %gather_fusion = f32[4096,3]{1,0:T(8,128)S(1)} fusion(f32[3,32768]{0,1:T(8,128)} %bitcast.414, s32[4096]{0:T(1024)S(1)} %get-tuple-element.69), kind=kCustom, calls=%fused_computation | custom fusion | bytes 114688 | tf_op jit(solution)/shard_map/jvp()/gather | solution.py:168
  178.8 40.6 %gather_fusion.3 = f32[4096]{0:T(1024)} fusion(f32[32768]{0:T(1024)S(1)} %bitcast.407, s32[4096]{0:T(1024)S(1)} %get-tuple-element.69), kind=kCustom, calls=%fused_computation.3 | custom fusion | bytes 49152 | tf_op jit(solution)/shard_map/jvp()/gather | solution.py:168
  219.4 23.0 %gather_fusion.1 = f32[4096]{0:T(1024)S(1)} fusion(f32[32768]{0:T(1024)S(1)} %bitcast.408, s32[4096]{0:T(1024)S(1)} %get-tuple-element.69), kind=kCustom, calls=%fused_computation.1 | custom fusion | bytes 49152 | tf_op jit(solution)/shard_map/jvp()/gather | solution.py:168
  242.4 36.5 %scatter_custom_fusion = f32[3,32768]{0,1:T(8,128)} fusion(f32[3,32768]{0,1:T(8,128)} %bitcast.409, s32[4096]{0:T(1024)} %bitcast.429, f32[4096,3]{1,0:T(8,128)S(1)} %gather_fusion, f32[4096]{0:T(1024)S(1)} %bitcast.419, f32[4096]{0:T(1024)S(1)} %bitcast.417), kind=kCustom, calls=%fused_computation.15 | custom fusion | flops 36864 | bytes 475136 | tf_op jit(solution)/shard_map/jvp()/scatter-add | solution.py:172
  278.9 10.7 %copy.115 = f32[3,2,128,128]{3,2,1,0:T(8,128)} copy(f32[3,2,128,128]{0,3,2,1:T(8,128)} %bitcast.410) | data formatting | bytes 786432
  289.6 2.5 fusion.31
  292.1 9.5 %copy.111 = f32[3,2,128,128]{0,3,2,1:T(8,128)} copy(f32[3,2,128,128]{3,2,1,0:T(8,128)} %fusion.31) | data formatting | bytes 786432 | tf_op jit(solution)/shard_map/jvp()/sub | solution.py:163
  301.6 8.5 %copy.112 = f32[3,2,128,128]{0,3,2,1:T(8,128)} copy(f32[3,2,128,128]{3,2,1,0:T(8,128)S(1)} %get-tuple-element.105) | data formatting | bytes 786432 | tf_op jit(solution)/shard_map/jvp()/slice | solution.py:133
  310.1 19.9 %gather_fusion.2 = f32[4096,3]{1,0:T(8,128)} fusion(f32[3,32768]{0,1:T(8,128)} %bitcast.415, s32[4096]{0:T(1024)S(1)} %get-tuple-element.69), kind=kCustom, calls=%fused_computation.2 | custom fusion | bytes 114688 | tf_op jit(solution)/shard_map/jvp()/gather | solution.py:168
  330.1 37.0 %scatter_custom_fusion.1 = f32[3,32768]{0,1:T(8,128)} fusion(f32[3,32768]{0,1:T(8,128)} %bitcast.411, s32[4096]{0:T(1024)} %bitcast.430, f32[4096,3]{1,0:T(8,128)} %gather_fusion.2, f32[4096,3]{1,0:T(8,128)S(1)} %gather_fusion, f32[4096]{0:T(1024)S(1)} %bitcast.425, f32[4096]{0:T(1024)S(1)} %bitcast.420, f32[4096]{0:T(1024)S(1)} %bitcast.418), kind=kCustom, calls=%fused_computation.13 | custom fusion | flops 73728 | bytes 2588672 | tf_op jit(solution)/shard_map/jvp()/scatter-add | solution.py:172
  367.0 10.6 %copy.116 = f32[3,2,128,128]{3,2,1,0:T(8,128)} copy(f32[3,2,128,128]{0,3,2,1:T(8,128)} %bitcast.412) | data formatting | bytes 786432
  377.7 4.6 add_reduce_fusion
  382.4 46.0 %all-reduce.4 = (f32[32,128]{1,0:T(8,128)S(1)}, f32[32,128]{1,0:T(8,128)S(1)}) all-reduce(f32[32,128]{1,0:T(8,128)S(1)} %get-tuple-element.55, f32[32,128]{1,0:T(8,128)S(1)} %get-tuple-element.54), channel_id=1, replica_groups=mesh['gx'=16,'gy'=16] {'gy'}, use_global_device_ids=true, to_apply=%region_3.4 | all-reduce | flops 8192 | bytes 65536 | tf_op jit(solution)/shard_map/psum | solution.py:201
  430.2 1.7 fusion.174
  435.5 75.3 %psum.31 = f32[3,128]{1,0:T(4,128)} all-reduce(f32[3,128]{1,0:T(4,128)S(1)} %fusion.157), channel_id=1, replica_groups=mesh['gx'=16,'gy'=16] {'gx','gy'}, use_global_device_ids=true, to_apply=%region_9.10 | all-reduce | flops 384 | bytes 3072 | tf_op jit(solution)/shard_map/psum | solution.py:188
  (113 shorter events, 28.2 us)
Async XLA Ops:
  0.6 431.5 %copy-start = (f32[128]{0:T(128)S(1)}, f32[128]{0:T(128)}, u32[]{:S(2)}) copy-start(f32[128]{0:T(128)} %param.37) | copy-start | bytes 1540
  0.6 10.9 %copy-start.8 = (s32[32,128]{1,0:T(8,128)S(1)}, s32[32,128]{1,0:T(8,128)}, u32[]{:S(2)}) copy-start(s32[32,128]{1,0:T(8,128)} %param.29) | copy-start | bytes 49156
  0.7 11.5 %copy-start.12 = (f32[32,128]{1,0:T(8,128)S(1)}, f32[32,128]{1,0:T(8,128)}, u32[]{:S(2)}) copy-start(f32[32,128]{1,0:T(8,128)} %param.30) | copy-start | bytes 49156
  0.7 11.5 %copy-start.9 = (s32[32,128]{1,0:T(8,128)S(1)}, s32[32,128]{1,0:T(8,128)}, u32[]{:S(2)}) copy-start(s32[32,128]{1,0:T(8,128)} %param.31) | copy-start | bytes 49156
  5.6 45.2 %collective-permute-start.1 = (f32[8,2,1,128]{3,2,1,0:T(1,128)S(1)}, f32[8,2,1,128]{3,2,1,0:T(1,128)S(1)}, u32[]{:S(2)}, u32[]{:S(2)}) collective-permute-start(f32[8,2,1,128]{3,2,1,0:T(1,128)S(1)} %get-tuple-element.89), channel_id=1, source_target_pairs={{16,0},{32,16},{48,32},{64,48},{80,64},{96,80},{112,96},{128,112},... | collective-permute-start | bytes 24584 | tf_op jit(solution)/shard_map/ppermute | solution.py:24
  6.9 43.9 %collective-permute-start = (f32[8,2,1,128]{3,2,1,0:T(1,128)S(1)}, f32[8,2,1,128]{3,2,1,0:T(1,128)S(1)}, u32[]{:S(2)}, u32[]{:S(2)}) collective-permute-start(f32[8,2,1,128]{3,2,1,0:T(1,128)S(1)} %get-tuple-element.88), channel_id=1, source_target_pairs={{0,16},{16,32},{32,48},{48,64},{64,80},{80,96},{96,112},{112,128},... | collective-permute-start | bytes 24584 | tf_op jit(solution)/shard_map/ppermute | solution.py:23
  15.0 2.0 copy-start.16
  15.0 2.0 copy-start.19
  15.0 35.2 %copy-start.2 = (f32[32,128]{1,0:T(8,128)S(1)}, f32[32,128]{1,0:T(8,128)}, u32[]{:S(2)}) copy-start(f32[32,128]{1,0:T(8,128)} %param.27) | copy-start | bytes 49156
  51.3 14.8 %copy-start.1 = (f32[32,128]{1,0:T(8,128)S(1)}, f32[32,128]{1,0:T(8,128)}, u32[]{:S(2)}) copy-start(f32[32,128]{1,0:T(8,128)} %param.28) | copy-start | bytes 49156
  51.9 83.8 %collective-permute-start.3 = (f32[8,2,130,1]{2,0,3,1:T(8,128)S(1)}, f32[8,2,130,1]{2,0,3,1:T(8,128)S(1)}, u32[]{:S(2)}, u32[]{:S(2)}) collective-permute-start(f32[8,2,130,1]{2,0,3,1:T(8,128)S(1)} %copy.106), channel_id=1, source_target_pairs={{1,0},{2,1},{3,2},{4,3},{5,4},{6,5},{7,6},{8,7},{9,8},{10,9},{11,1... | collective-permute-start | bytes 24968 | tf_op jit(solution)/shard_map/ppermute | solution.py:24
  62.4 73.7 %collective-permute-start.2 = (f32[8,2,130,1]{2,0,3,1:T(8,128)S(1)}, f32[8,2,130,1]{2,0,3,1:T(8,128)S(1)}, u32[]{:S(2)}, u32[]{:S(2)}) collective-permute-start(f32[8,2,130,1]{2,0,3,1:T(8,128)S(1)} %copy.105), channel_id=1, source_target_pairs={{0,1},{1,2},{2,3},{3,4},{4,5},{5,6},{6,7},{7,8},{8,9},{9,10},{10,1... | collective-permute-start | bytes 24968 | tf_op jit(solution)/shard_map/ppermute | solution.py:23
  143.0 1.8 copy-start.6
  219.4 23.0 %copy-start.11 = (f32[4096]{0:T(1024)S(1)}, f32[4096]{0:T(1024)}, u32[]{:S(2)}) copy-start(f32[4096]{0:T(1024)} %gather_fusion.3) | copy-start | bytes 49156
  278.9 10.7 %copy-start.4 = (f32[3,1,128,128]{3,2,1,0:T(8,128)S(1)}, f32[3,1,128,128]{3,2,1,0:T(8,128)}, u32[]{:S(2)}) copy-start(f32[3,1,128,128]{3,2,1,0:T(8,128)} %get-tuple-element.112) | copy-start | bytes 589828
  377.7 50.7 %copy-start.3 = (bf16[32,128,128]{2,1,0:T(8,128)(2,1)S(1)}, bf16[32,128,128]{2,1,0:T(8,128)(2,1)}, u32[]{:S(2)}) copy-start(bf16[32,128,128]{2,1,0:T(8,128)(2,1)} %minimum_convert_fusion) | copy-start | bytes 3145732
  377.7 52.5 %copy-start.10 = (f32[4096]{0:T(1024)S(1)}, f32[4096]{0:T(1024)}, u32[]{:S(2)}) copy-start(f32[4096]{0:T(1024)} %gather_fusion.5) | copy-start | bytes 49156
  382.3 49.8 %copy-start.14 = (f32[32]{0:T(128)S(1)}, f32[32]{0:T(128)}, u32[]{:S(2)}) copy-start(f32[32]{0:T(128)} %slice_reduce_fusion.2) | copy-start | bytes 388
  382.3 49.8 %copy-start.15 = (s32[32]{0:T(128)S(1)}, s32[32]{0:T(128)}, u32[]{:S(2)}) copy-start(s32[32]{0:T(128)} %param.33) | copy-start | bytes 388
  382.3 49.8 %copy-start.17 = (f32[32]{0:T(128)S(1)}, f32[32]{0:T(128)}, u32[]{:S(2)}) copy-start(f32[32]{0:T(128)} %param.35) | copy-start | bytes 388
  382.3 49.8 %copy-start.18 = (f32[32]{0:T(128)S(1)}, f32[32]{0:T(128)}, u32[]{:S(2)}) copy-start(f32[32]{0:T(128)} %param.34) | copy-start | bytes 388
  382.4 49.8 %copy-start.20 = (s32[32,1]{0,1:T(1,128)S(1)}, s32[32,1]{0,1:T(1,128)}, u32[]{:S(2)}) copy-start(s32[32,1]{0,1:T(1,128)} %param.36) | copy-start | bytes 388
  382.4 49.8 %copy-start.21 = (f32[32]{0:T(128)S(1)}, f32[32]{0:T(128)}, u32[]{:S(2)}) copy-start(f32[32]{0:T(128)} %convolution_bitcast_fusion) | copy-start | bytes 388
  382.4 50.1 %copy-start.13 = (f32[32,128]{1,0:T(8,128)S(1)}, f32[32,128]{1,0:T(8,128)}, u32[]{:S(2)}) copy-start(f32[32,128]{1,0:T(8,128)} %param.32) | copy-start | bytes 49156
  (2 other events, 3.0 us)
where the time goes:
time: 512 us; the launch traced here: 511 us
  local copies, waits for them, and re-layouts  233 us (46%)
  blocking collectives  154 us (30%)
  other arithmetic  93.7 us (18%)
  starting transfers between devices  19.4 us (4%)
  matrix products  9.4 us (2%)
    psum x1, blocking collectives, per_device(): group_rates = lax.psum(rates_part, ('gx', 'gy'))  75.3 us
    scatter-add x2, other arithmetic, local_terms(): residual = residual.reshape(3, -1).at[:, flat_cell.reshape(-1)].add(rates...  73.5 us
    gather x2, local copies, waits for them, and re-layouts, equations(): above = jnp.take_along_axis(seg_vals, parent, axis=1)  68.8 us
    gather x2, local copies, waits for them, and re-layouts, local_terms(): press_in.reshape(-1)[flat_cell] - seg_vals  63.6 us
    psum x1, blocking collectives, per_device(): total_sum, tangent_sum = lax.psum((rate_total, total_tangent), 'gy')  46 us
    gather x2, local copies, waits for them, and re-layouts, local_terms(): mobil_flat[:, flat_cell]  36.5 us
    psum x1, blocking collectives, per_device(): guide_total = lax.psum(guide_part, 'gx')  32.3 us
    unnamed x49, local copies, waits for them, and re-layouts  24.4 us
  transfers between devices with their start and end apart: 4, of which 0 were waited for; matrix products, arithmetic and copies ran while one was open for 15% of the time, Pallas kernels for 0%

commit v1 on v0

--- a/solution.py
+++ b/solution.py
@@ -2,6 +2,7 @@
 import jax.numpy as jnp
 from jax import lax
 from jax.sharding import PartitionSpec as P
+from jax.lax import all_gather
 
 COMPRESS = (0.05, 0.2, 1.0)
 VISCOSITY = (0.5, 1.0, 0.2)
@@ -184,7 +185,7 @@
     ).astype(jnp.float32)
     rates_part = jnp.dot(jnp.sum(rates, axis=2), member, precision=lax.Precision.HIGHEST)
     guide_part = jnp.dot(guide_rate, member, precision=lax.Precision.HIGHEST)
-    guide_total = lax.psum(guide_part, "gx")
+    guide_total = all_gather(guide_part, "gx").sum(axis=0)
     group_rates = lax.psum(rates_part, ("gx", "gy"))
     target = (
         jnp.dot(member, group_target, precision=lax.Precision.HIGHEST)

time: 512 us -> 497 us (0.971)
  blocking collectives: 154 us -> 141 us
    psum x1 -> x0, blocking collectives: 32.3 us -> none  [per_device(): guide_total = lax.psum(guide_part, 'gx')]
    all_gather x0 -> x1, blocking collectives: none -> 18.6 us  [per_device(): guide_total = all_gather(guide_part, 'gx').sum(axis=0)]
  transfers between devices with their start and end apart: 4 -> 4, of which waited for: 0 -> 0; matrix products, arithmetic and copies ran while one was open for 15% -> 16% of each run, Pallas kernels for 0% -> 0%
where the time goes in v1:
time: 497 us; the launch traced here: 496 us
  local copies, waits for them, and re-layouts  233 us (47%)
  blocking collectives  141 us (28%)
  other arithmetic  93.7 us (19%)
  starting transfers between devices  17.2 us (3%)
  matrix products  9.4 us (2%)
    psum x1, blocking collectives, per_device(): group_rates = lax.psum(rates_part, ('gx', 'gy'))  76.6 us
    scatter-add x2, other arithmetic, local_terms(): residual = residual.reshape(3, -1).at[:, flat_cell.reshape(-1)].add(rates...  73.5 us
    gather x2, local copies, waits for them, and re-layouts, equations(): above = jnp.take_along_axis(seg_vals, parent, axis=1)  68.8 us
    gather x2, local copies, waits for them, and re-layouts, local_terms(): press_in.reshape(-1)[flat_cell] - seg_vals  63.6 us
    psum x1, blocking collectives, per_device(): total_sum, tangent_sum = lax.psum((rate_total, total_tangent), 'gy')  46 us
    gather x2, local copies, waits for them, and re-layouts, local_terms(): mobil_flat[:, flat_cell]  36.5 us
    unnamed x49, local copies, waits for them, and re-layouts  24.4 us
    all_gather x1, blocking collectives, per_device(): guide_total = all_gather(guide_part, 'gx').sum(axis=0)  18.6 us
  transfers between devices with their start and end apart: 4, of which 0 were waited for; matrix products, arithmetic and copies ran while one was open for 16% of the time, Pallas kernels for 0%

profile of v1, /device:TPU:1, one launch (start us, length us, event | category | flops | bytes accessed | tf_op | source)
XLA Modules:
  0.0 496.1 jit_solution(18124536446943893853)
XLA Ops:
  6.9 4.6 collective-permute-start
  15.0 2.0 minimum_convert_fusion
  17.2 18.6 %all-gather.1 = f32[16,1,128]{2,1,0:T(1,128)S(1)} all-gather(f32[1,1,128]{2,1,0:T(1,128)S(1)} %convolution_bitcast_fusion.1), channel_id=2, replica_groups=mesh['gx'=16,'gy'=16] {'gx'}, dimensions={0}, use_global_device_ids=true | all-gather | bytes 8704 | tf_op jit(solution)/shard_map/all_gather | solution.py:188
  38.2 7.7 %collective-permute-start.3 = (f32[8,2,130,1]{2,0,3,1:T(8,128)S(1)}, f32[8,2,130,1]{2,0,3,1:T(8,128)S(1)}, u32[]{:S(2)}, u32[]{:S(2)}) collective-permute-start(f32[8,2,130,1]{2,0,3,1:T(8,128)S(1)} %copy.106), channel_id=1, source_target_pairs={{1,0},{2,1},{3,2},{4,3},{5,4},{6,5},{7,6},{8,7},{9,8},{10,9},{11,1... | collective-permute-start | bytes 24968 | tf_op jit(solution)/shard_map/ppermute | solution.py:25
  46.5 3.6 collective-permute-start.2
  50.3 43.2 %gather_fusion.5 = f32[4096]{0:T(1024)} fusion(f32[32,128]{1,0:T(8,128)S(1)} %copy-done.1, s32[4096]{0:T(1024)S(1)} %fusion.156), kind=kCustom, calls=%fused_computation.5 | custom fusion | bytes 65536 | tf_op jit(solution)/shard_map/jvp(jit(take_along_axis))/gather | solution.py:72
  93.5 25.6 %gather_fusion.4 = f32[4096]{0:T(1024)S(1)} fusion(f32[32,128]{1,0:T(8,128)S(1)} %copy-done.2, s32[4096]{0:T(1024)S(1)} %fusion.156), kind=kCustom, calls=%fused_computation.4 | custom fusion | bytes 65536 | tf_op jit(solution)/shard_map/jvp(jit(take_along_axis))/gather | solution.py:72
  129.3 8.6 %copy.109 = f32[3,2,128,128]{0,3,2,1:T(8,128)} copy(f32[3,2,128,128]{3,2,1,0:T(8,128)S(1)} %fusion.34) | data formatting | bytes 786432 | tf_op jit(solution)/shard_map/jvp()/sub | solution.py:164
  137.8 8.5 %copy.110 = f32[3,2,128,128]{0,3,2,1:T(8,128)} copy(f32[3,2,128,128]{3,2,1,0:T(8,128)S(1)} %get-tuple-element.106) | data formatting | bytes 786432 | tf_op jit(solution)/shard_map/jvp()/slice | solution.py:134
  146.3 16.5 %gather_fusion = f32[4096,3]{1,0:T(8,128)S(1)} fusion(f32[3,32768]{0,1:T(8,128)} %bitcast.416, s32[4096]{0:T(1024)S(1)} %get-tuple-element.69), kind=kCustom, calls=%fused_computation | custom fusion | bytes 114688 | tf_op jit(solution)/shard_map/jvp()/gather | solution.py:169
  162.9 40.6 %gather_fusion.3 = f32[4096]{0:T(1024)} fusion(f32[32768]{0:T(1024)S(1)} %bitcast.409, s32[4096]{0:T(1024)S(1)} %get-tuple-element.69), kind=kCustom, calls=%fused_computation.3 | custom fusion | bytes 49152 | tf_op jit(solution)/shard_map/jvp()/gather | solution.py:169
  203.5 23.0 %gather_fusion.1 = f32[4096]{0:T(1024)S(1)} fusion(f32[32768]{0:T(1024)S(1)} %bitcast.410, s32[4096]{0:T(1024)S(1)} %get-tuple-element.69), kind=kCustom, calls=%fused_computation.1 | custom fusion | bytes 49152 | tf_op jit(solution)/shard_map/jvp()/gather | solution.py:169
  226.5 36.5 %scatter_custom_fusion = f32[3,32768]{0,1:T(8,128)} fusion(f32[3,32768]{0,1:T(8,128)} %bitcast.411, s32[4096]{0:T(1024)} %bitcast.431, f32[4096,3]{1,0:T(8,128)S(1)} %gather_fusion, f32[4096]{0:T(1024)S(1)} %bitcast.421, f32[4096]{0:T(1024)S(1)} %bitcast.419), kind=kCustom, calls=%fused_computation.15 | custom fusion | flops 36864 | bytes 475136 | tf_op jit(solution)/shard_map/jvp()/scatter-add | solution.py:173
  263.0 10.7 %copy.115 = f32[3,2,128,128]{3,2,1,0:T(8,128)} copy(f32[3,2,128,128]{0,3,2,1:T(8,128)} %bitcast.412) | data formatting | bytes 786432
  273.7 2.5 fusion.31
  276.2 9.5 %copy.111 = f32[3,2,128,128]{0,3,2,1:T(8,128)} copy(f32[3,2,128,128]{3,2,1,0:T(8,128)} %fusion.31) | data formatting | bytes 786432 | tf_op jit(solution)/shard_map/jvp()/sub | solution.py:164
  285.7 8.5 %copy.112 = f32[3,2,128,128]{0,3,2,1:T(8,128)} copy(f32[3,2,128,128]{3,2,1,0:T(8,128)S(1)} %get-tuple-element.105) | data formatting | bytes 786432 | tf_op jit(solution)/shard_map/jvp()/slice | solution.py:134
  294.2 19.9 %gather_fusion.2 = f32[4096,3]{1,0:T(8,128)} fusion(f32[3,32768]{0,1:T(8,128)} %bitcast.417, s32[4096]{0:T(1024)S(1)} %get-tuple-element.69), kind=kCustom, calls=%fused_computation.2 | custom fusion | bytes 114688 | tf_op jit(solution)/shard_map/jvp()/gather | solution.py:169
  314.2 37.0 %scatter_custom_fusion.1 = f32[3,32768]{0,1:T(8,128)} fusion(f32[3,32768]{0,1:T(8,128)} %bitcast.413, s32[4096]{0:T(1024)} %bitcast.432, f32[4096,3]{1,0:T(8,128)} %gather_fusion.2, f32[4096,3]{1,0:T(8,128)S(1)} %gather_fusion, f32[4096]{0:T(1024)S(1)} %bitcast.427, f32[4096]{0:T(1024)S(1)} %bitcast.422, f32[4096]{0:T(1024)S(1)} %bitcast.420), kind=kCustom, calls=%fused_computation.13 | custom fusion | flops 73728 | bytes 2588672 | tf_op jit(solution)/shard_map/jvp()/scatter-add | solution.py:173
  351.1 10.6 %copy.116 = f32[3,2,128,128]{3,2,1,0:T(8,128)} copy(f32[3,2,128,128]{0,3,2,1:T(8,128)} %bitcast.414) | data formatting | bytes 786432
  361.8 4.6 add_reduce_fusion
  366.5 46.0 %all-reduce.4 = (f32[32,128]{1,0:T(8,128)S(1)}, f32[32,128]{1,0:T(8,128)S(1)}) all-reduce(f32[32,128]{1,0:T(8,128)S(1)} %get-tuple-element.55, f32[32,128]{1,0:T(8,128)S(1)} %get-tuple-element.54), channel_id=1, replica_groups=mesh['gx'=16,'gy'=16] {'gy'}, use_global_device_ids=true, to_apply=%region_3.4 | all-reduce | flops 8192 | bytes 65536 | tf_op jit(solution)/shard_map/psum | solution.py:202
  414.3 1.7 fusion.174
  419.6 76.6 %psum.23 = f32[3,128]{1,0:T(4,128)} all-reduce(f32[3,128]{1,0:T(4,128)S(1)} %fusion.157), channel_id=1, replica_groups=mesh['gx'=16,'gy'=16] {'gx','gy'}, use_global_device_ids=true, to_apply=%region_9.10 | all-reduce | flops 384 | bytes 3072 | tf_op jit(solution)/shard_map/psum | solution.py:189
  (114 shorter events, 28.3 us)
Async XLA Ops:
  0.6 415.5 %copy-start = (f32[128]{0:T(128)S(1)}, f32[128]{0:T(128)}, u32[]{:S(2)}) copy-start(f32[128]{0:T(128)} %param.37) | copy-start | bytes 1540
  0.6 10.9 %copy-start.8 = (s32[32,128]{1,0:T(8,128)S(1)}, s32[32,128]{1,0:T(8,128)}, u32[]{:S(2)}) copy-start(s32[32,128]{1,0:T(8,128)} %param.29) | copy-start | bytes 49156
  0.7 11.5 %copy-start.12 = (f32[32,128]{1,0:T(8,128)S(1)}, f32[32,128]{1,0:T(8,128)}, u32[]{:S(2)}) copy-start(f32[32,128]{1,0:T(8,128)} %param.30) | copy-start | bytes 49156
  0.7 11.5 %copy-start.9 = (s32[32,128]{1,0:T(8,128)S(1)}, s32[32,128]{1,0:T(8,128)}, u32[]{:S(2)}) copy-start(s32[32,128]{1,0:T(8,128)} %param.31) | copy-start | bytes 49156
  5.6 31.5 %collective-permute-start.1 = (f32[8,2,1,128]{3,2,1,0:T(1,128)S(1)}, f32[8,2,1,128]{3,2,1,0:T(1,128)S(1)}, u32[]{:S(2)}, u32[]{:S(2)}) collective-permute-start(f32[8,2,1,128]{3,2,1,0:T(1,128)S(1)} %get-tuple-element.89), channel_id=1, source_target_pairs={{16,0},{32,16},{48,32},{64,48},{80,64},{96,80},{112,96},{128,112},... | collective-permute-start | bytes 24584 | tf_op jit(solution)/shard_map/ppermute | solution.py:25
  6.9 30.2 %collective-permute-start = (f32[8,2,1,128]{3,2,1,0:T(1,128)S(1)}, f32[8,2,1,128]{3,2,1,0:T(1,128)S(1)}, u32[]{:S(2)}, u32[]{:S(2)}) collective-permute-start(f32[8,2,1,128]{3,2,1,0:T(1,128)S(1)} %get-tuple-element.88), channel_id=1, source_target_pairs={{0,16},{16,32},{32,48},{48,64},{64,80},{80,96},{96,112},{112,128},... | collective-permute-start | bytes 24584 | tf_op jit(solution)/shard_map/ppermute | solution.py:24
  15.0 2.0 copy-start.16
  15.0 2.0 copy-start.19
  15.0 21.5 %copy-start.2 = (f32[32,128]{1,0:T(8,128)S(1)}, f32[32,128]{1,0:T(8,128)}, u32[]{:S(2)}) copy-start(f32[32,128]{1,0:T(8,128)} %param.27) | copy-start | bytes 49156
  37.6 12.6 %copy-start.1 = (f32[32,128]{1,0:T(8,128)S(1)}, f32[32,128]{1,0:T(8,128)}, u32[]{:S(2)}) copy-start(f32[32,128]{1,0:T(8,128)} %param.28) | copy-start | bytes 49156
  38.2 81.6 %collective-permute-start.3 = (f32[8,2,130,1]{2,0,3,1:T(8,128)S(1)}, f32[8,2,130,1]{2,0,3,1:T(8,128)S(1)}, u32[]{:S(2)}, u32[]{:S(2)}) collective-permute-start(f32[8,2,130,1]{2,0,3,1:T(8,128)S(1)} %copy.106), channel_id=1, source_target_pairs={{1,0},{2,1},{3,2},{4,3},{5,4},{6,5},{7,6},{8,7},{9,8},{10,9},{11,1... | collective-permute-start | bytes 24968 | tf_op jit(solution)/shard_map/ppermute | solution.py:25
  46.5 73.7 %collective-permute-start.2 = (f32[8,2,130,1]{2,0,3,1:T(8,128)S(1)}, f32[8,2,130,1]{2,0,3,1:T(8,128)S(1)}, u32[]{:S(2)}, u32[]{:S(2)}) collective-permute-start(f32[8,2,130,1]{2,0,3,1:T(8,128)S(1)} %copy.105), channel_id=1, source_target_pairs={{0,1},{1,2},{2,3},{3,4},{4,5},{5,6},{6,7},{7,8},{8,9},{9,10},{10,1... | collective-permute-start | bytes 24968 | tf_op jit(solution)/shard_map/ppermute | solution.py:24
  127.1 1.8 copy-start.6
  203.4 23.0 %copy-start.11 = (f32[4096]{0:T(1024)S(1)}, f32[4096]{0:T(1024)}, u32[]{:S(2)}) copy-start(f32[4096]{0:T(1024)} %gather_fusion.3) | copy-start | bytes 49156
  263.0 10.7 %copy-start.4 = (f32[3,1,128,128]{3,2,1,0:T(8,128)S(1)}, f32[3,1,128,128]{3,2,1,0:T(8,128)}, u32[]{:S(2)}) copy-start(f32[3,1,128,128]{3,2,1,0:T(8,128)} %get-tuple-element.112) | copy-start | bytes 589828
  361.8 50.7 %copy-start.3 = (bf16[32,128,128]{2,1,0:T(8,128)(2,1)S(1)}, bf16[32,128,128]{2,1,0:T(8,128)(2,1)}, u32[]{:S(2)}) copy-start(bf16[32,128,128]{2,1,0:T(8,128)(2,1)} %minimum_convert_fusion) | copy-start | bytes 3145732
  361.8 52.5 %copy-start.10 = (f32[4096]{0:T(1024)S(1)}, f32[4096]{0:T(1024)}, u32[]{:S(2)}) copy-start(f32[4096]{0:T(1024)} %gather_fusion.5) | copy-start | bytes 49156
  366.4 49.8 %copy-start.14 = (f32[32]{0:T(128)S(1)}, f32[32]{0:T(128)}, u32[]{:S(2)}) copy-start(f32[32]{0:T(128)} %slice_reduce_fusion.2) | copy-start | bytes 388
  366.4 49.8 %copy-start.15 = (s32[32]{0:T(128)S(1)}, s32[32]{0:T(128)}, u32[]{:S(2)}) copy-start(s32[32]{0:T(128)} %param.33) | copy-start | bytes 388
  366.4 49.8 %copy-start.17 = (f32[32]{0:T(128)S(1)}, f32[32]{0:T(128)}, u32[]{:S(2)}) copy-start(f32[32]{0:T(128)} %param.35) | copy-start | bytes 388
  366.4 49.8 %copy-start.18 = (f32[32]{0:T(128)S(1)}, f32[32]{0:T(128)}, u32[]{:S(2)}) copy-start(f32[32]{0:T(128)} %param.34) | copy-start | bytes 388
  366.4 49.8 %copy-start.20 = (s32[32,1]{0,1:T(1,128)S(1)}, s32[32,1]{0,1:T(1,128)}, u32[]{:S(2)}) copy-start(s32[32,1]{0,1:T(1,128)} %param.36) | copy-start | bytes 388
  366.5 49.8 %copy-start.21 = (f32[32]{0:T(128)S(1)}, f32[32]{0:T(128)}, u32[]{:S(2)}) copy-start(f32[32]{0:T(128)} %convolution_bitcast_fusion) | copy-start | bytes 388
  366.5 50.1 %copy-start.13 = (f32[32,128]{1,0:T(8,128)S(1)}, f32[32,128]{1,0:T(8,128)}, u32[]{:S(2)}) copy-start(f32[32,128]{1,0:T(8,128)} %param.32) | copy-start | bytes 49156
  (2 other events, 3.0 us)
